TPU v7x, 512 devices: a whole 4x8x8 slice. The times are simulated.
512 devices in a mesh: gx: 8 (over z), gy: 8 (over y_lo, x), gz: 8 (over y_hi, core).
Axes of the slice: x: 4, y: 8 (y_hi: 4, y_lo: 2; y = y_hi * 2 + y_lo), z: 8, core: 2. Of those that a mesh axis runs over, the one named last changes fastest.
Arguments:
- tokens: bfloat16 [2048, 8192], P('gy', ('gz', 'gx')), may hold values from -6 to 6
- gate_weight: bfloat16 [8192, 14336], P(('gz', 'gy'), 'gx'), may hold values from -0.0625 to 0.0625
- up_weight: bfloat16 [8192, 14336], P(('gz', 'gy'), 'gx'), may hold values from -0.0625 to 0.0625
- down_weight: bfloat16 [14336, 8192], P(('gx', 'gy'), 'gz'), may hold values from -0.046875 to 0.046875
Outputs:
- ffn_out: bfloat16 [2048, 8192], P('gy', ('gz', 'gx'))
All inputs are finite; a program needn't handle non-finite values.
Results may differ from a plain program's by a relative error of at most 0.019.
Values may be sent and summed in bfloat16 or wider, within the bound.
A program may use at most 64 MiB of HBM per device.

v0:
```python
import jax
import jax.numpy as jnp
from jax import lax
from jax.sharding import PartitionSpec as P


def local(tokens, gate_weight, up_weight, down_weight):
    token_block = lax.all_gather(tokens, "gx", axis=1, tiled=True)
    columns = token_block
    gate_next = jnp.dot(
        columns,
        lax.all_gather(gate_weight, "gy", axis=0, tiled=True),
        preferred_element_type=jnp.float32,
    )
    up_next = jnp.dot(
        columns,
        lax.all_gather(up_weight, "gy", axis=0, tiled=True),
        preferred_element_type=jnp.float32,
    )
    gate_part, up_part = (
        lax.psum_scatter(gate_next, "gz", scatter_dimension=0, tiled=True),
        lax.psum_scatter(up_next, "gz", scatter_dimension=0, tiled=True),
    )
    local_hidden = (jax.nn.silu(gate_part) * up_part).astype(jnp.bfloat16)
    hidden = lax.all_gather(local_hidden, "gz", axis=0, tiled=True)
    columns = hidden
    partial_out = jnp.dot(
        columns,
        lax.all_gather(down_weight, "gy", axis=0, tiled=True),
        preferred_element_type=jnp.float32,
    )
    return lax.psum_scatter(partial_out.astype(jnp.bfloat16), "gx", scatter_dimension=1, tiled=True)


def solution(mesh):
    in_specs = (
        P("gy", ("gz", "gx")),
        P(("gz", "gy"), "gx"),
        P(("gz", "gy"), "gx"),
        P(("gx", "gy"), "gz"),
    )
    out_specs = P("gy", ("gz", "gx"))
    return jax.shard_map(local, mesh=mesh, in_specs=in_specs, out_specs=out_specs, check_vma=False)
```

profile of v0, /device:TPU:1, one launch (start us, length us, event | category | flops | bytes accessed | tf_op | source)
XLA Modules:
  0.0 319.5 jit_solution(11553099294541293481)
XLA Ops:
  6.5 0.0 all-gather.4.cloned.1.call-start
  6.5 0.7 all-gather.4.cloned.1.call-update
  7.3 0.0 all-gather.6.cloned.1.call-start
  7.3 0.7 all-gather.6.cloned.1.call-update
  8.0 0.0 reduce-scatter.6.cloned.1.call-start
  8.1 26.5 %all_gather.15 = bf16[256,1024]{1,0:T(8,128)(2,1)S(1)} all-gather(bf16[256,128]{1,0:T(8,128)(2,1)} %param.4), channel_id=1, replica_groups=mesh['gx'=8,'gy'=8,'gz'=8] {'gx'}, dimensions={1}, use_global_device_ids=true | all-gather | bytes 589824 | tf_op jit(solution)/shard_map/all_gather | solution.py:8
  34.6 33.4 %all-gather.4.cloned.1.call-done = bf16[1024,1792]{1,0:T(8,128)(2,1)} async-done(((bf16[128,1792]{1,0:T(8,128)(2,1)}), bf16[1024,1792]{1,0:T(8,128)(2,1)}) %all-gather.4.cloned.1.call-update) | async-done | bytes 3670032 | tf_op jit(solution)/shard_map/all_gather | solution.py:12
  68.0 4.4 %fusion = f32[256,1792]{1,0:T(8,128)} fusion(bf16[256,1024]{1,0:T(8,128)(2,1)S(1)} %all_gather.15, bf16[1024,1792]{1,0:T(8,128)(2,1)} %all-gather.4.cloned.1.call-done), kind=kOutput, calls=%fused_computation.2 | convolution fusion | flops 939524096 | bytes 6029312 | tf_op jit(solution)/shard_map/dot_general | solution.py:10
  72.4 0.0 reduce-scatter.6.cloned.1.call-update
  72.4 0.0 reduce-scatter.8.cloned.1.call-start
  72.5 49.9 %all-gather.6.cloned.1.call-done = bf16[1024,1792]{1,0:T(8,128)(2,1)} async-done(((bf16[128,1792]{1,0:T(8,128)(2,1)}), bf16[1024,1792]{1,0:T(8,128)(2,1)}) %all-gather.6.cloned.1.call-update) | async-done | bytes 3670032 | tf_op jit(solution)/shard_map/all_gather | solution.py:17
  122.4 4.4 %fusion.1 = f32[256,1792]{1,0:T(8,128)} fusion(bf16[256,1024]{1,0:T(8,128)(2,1)S(1)} %all_gather.15, bf16[1024,1792]{1,0:T(8,128)(2,1)} %all-gather.6.cloned.1.call-done), kind=kOutput, calls=%fused_computation.3 | convolution fusion | flops 939524096 | bytes 6029312 | tf_op jit(solution)/shard_map/dot_general | solution.py:15
  126.8 0.0 reduce-scatter.8.cloned.1.call-update
  126.9 0.0 all-gather.8.cloned.1.call-start
  126.9 0.5 all-gather.8.cloned.1.call-update
  127.5 0.0 reduce-scatter.10.cloned.1.call-start
  127.5 40.4 %reduce-scatter.6.cloned.1.call-done = f32[32,1792]{1,0:T(8,128)} async-done(((f32[256,1792]{1,0:T(8,128)}), f32[32,1792]{1,0:T(8,128)}) %reduce-scatter.6.cloned.1.call-update) | async-done | bytes 229392 | tf_op jit(solution)/shard_map/reduce_scatter | solution.py:21
  167.9 47.3 %reduce-scatter.8.cloned.1.call-done = f32[32,1792]{1,0:T(8,128)} async-done(((f32[256,1792]{1,0:T(8,128)}), f32[32,1792]{1,0:T(8,128)}) %reduce-scatter.8.cloned.1.call-update) | async-done | bytes 229392 | tf_op jit(solution)/shard_map/reduce_scatter | solution.py:22
  215.2 1.1 multiply_convert_fusion
  216.4 19.1 %all_gather.18 = bf16[256,1792]{1,0:T(8,128)(2,1)S(1)} all-gather(bf16[32,1792]{1,0:T(8,128)(2,1)S(1)} %multiply_convert_fusion), channel_id=1, replica_groups=mesh['gx'=8,'gy'=8,'gz'=8] {'gz'}, dimensions={0}, use_global_device_ids=true | all-gather | bytes 1032192 | tf_op jit(solution)/shard_map/all_gather | solution.py:25
  235.4 36.1 %all-gather.8.cloned.1.call-done = bf16[1792,1024]{1,0:T(8,128)(2,1)} async-done(((bf16[224,1024]{1,0:T(8,128)(2,1)}), bf16[1792,1024]{1,0:T(8,128)(2,1)}) %all-gather.8.cloned.1.call-update) | async-done | bytes 3670032 | tf_op jit(solution)/shard_map/all_gather | solution.py:29
  271.5 3.1 convolution_convert_fusion
  274.7 1.0 copy.5
  275.7 0.0 reduce-scatter.10.cloned.1.call-update
  275.7 35.4 %reduce-scatter.10.cloned.1.call-done = bf16[128,256]{1,0:T(8,128)(2,1)} async-done(((bf16[1024,256]{1,0:T(8,128)(2,1)}), bf16[128,256]{1,0:T(8,128)(2,1)}) %reduce-scatter.10.cloned.1.call-update) | async-done | bytes 65552
  311.1 1.6 copy.6
Async XLA Ops:
  6.5 61.4 %all-gather.4.cloned.1.call-start = ((), (), s32[]{:S(2)}) async-start(), calls=%async_computation.3 | async-start | bytes 4128768 | tf_op jit(solution)/shard_map/all_gather | solution.py:12
  7.3 115.2 %all-gather.6.cloned.1.call-start = ((), (), s32[]{:S(2)}) async-start(), calls=%async_computation.5 | async-start | bytes 4128768 | tf_op jit(solution)/shard_map/all_gather | solution.py:17
  8.0 159.9 %reduce-scatter.6.cloned.1.call-start = ((), (), s32[]{:S(2)}) async-start(), calls=%async_computation.4 | async-start | bytes 2064384 | tf_op jit(solution)/shard_map/reduce_scatter | solution.py:21
  72.4 142.8 %reduce-scatter.8.cloned.1.call-start = ((), (), s32[]{:S(2)}) async-start(), calls=%async_computation.6 | async-start | bytes 2064384 | tf_op jit(solution)/shard_map/reduce_scatter | solution.py:22
  126.9 144.7 %all-gather.8.cloned.1.call-start = ((), (), s32[]{:S(2)}) async-start(), calls=%async_computation.7 | async-start | bytes 4128768 | tf_op jit(solution)/shard_map/all_gather | solution.py:29
  127.5 183.7 %reduce-scatter.10.cloned.1.call-start = ((), (), s32[]{:S(2)}) async-start(), calls=%async_computation.8 | async-start | bytes 589824
Sparse Core Ops, SparseCore 0:
  9.4 58.4 all-gather.3
  70.0 52.3 all-gather.5
  125.3 42.5 reduce-scatter.5
  170.6 44.5 reduce-scatter.7
  217.2 54.3 all-gather.7
  275.8 35.2 reduce-scatter.9
where the time goes:
time: 324 us; the launch traced here: 320 us
  waiting for transfers between devices  245 us (76%)
  blocking collectives  45.6 us (14%)
  between operations  13.5 us (4%)
  matrix products  12 us (4%)
    all_gather x1, waiting for transfers between devices, local(): lax.all_gather(up_weight, 'gy', axis=0, tiled=True)  49.9 us
    reduce_scatter x1, waiting for transfers between devices, local(): lax.psum_scatter(up_next, 'gz', scatter_dimension=0, tiled=True)  47.3 us
    reduce_scatter x1, waiting for transfers between devices, local(): lax.psum_scatter(gate_next, 'gz', scatter_dimension=0, tiled=True)  40.4 us
    unnamed x7, waiting for transfers between devices  37.4 us
    all_gather x1, waiting for transfers between devices, local(): lax.all_gather(down_weight, 'gy', axis=0, tiled=True)  36.1 us
    all_gather x1, waiting for transfers between devices, local(): lax.all_gather(gate_weight, 'gy', axis=0, tiled=True)  33.4 us
    all_gather x1, blocking collectives, local(): token_block = lax.all_gather(tokens, 'gx', axis=1, tiled=True)  26.5 us
    all_gather x1, blocking collectives, local(): hidden = lax.all_gather(local_hidden, 'gz', axis=0, tiled=True)  19.1 us
  transfers between devices with their start and end apart: 6, of which 6 were waited for; matrix products, arithmetic and copies ran while one was open for 3% of the time, Pallas kernels for 0%

commit v1 on v0

v1 whole, which is shorter than its diff:
```python
import functools

import jax
import jax.numpy as jnp
from jax import lax
from jax.experimental import pallas as pl
from jax.experimental.pallas import tpu as pltpu
from jax.sharding import PartitionSpec as P

MESH = pl.DeviceIdType.MESH
F32, BF16 = jnp.float32, jnp.bfloat16
CHUNKS = 7
HALF = 896
ROWS = 224


def device(x, y, z, c):
    return (z, (y % 2) * 4 + x, (y // 2) * 2 + c)


def remote(src, dst, send, recv, target):
    copy = pltpu.make_async_remote_copy(
        src_ref=src, dst_ref=dst, send_sem=send, recv_sem=recv, device_id=target, device_id_type=MESH
    )
    copy.start()


def wait(ref, sem):
    pltpu.make_async_copy(ref, ref, sem).wait()


def kernel(
    tok_in, gate_in, up_in, down_in, out_ref,
    tok, wbuf, cbuf, s1, r1, sb, rb, hid, dbuf, osend, orecv,
    tok_sem, x_send, x_recv, f_send, ch_send, ch_recv, h_send, h1, h2, hs_send, hs_recv, d_sem, o_sem,
):
    z = lax.axis_index("gx")
    gy, gz = lax.axis_index("gy"), lax.axis_index("gz")
    x, ylo, yhi, c = gy % 4, gy // 4, gz // 2, gz % 2
    y = yhi * 2 + ylo
    right, left = (x + 1) % 4, (x + 3) % 4
    sibling = device(x, y, z, 1 - c)

    def at_y(step):
        return device(x, (y + 8 + step) % 8, z, c)

    peers = [device(n, y, z, k) for n in (left, right) for k in (0, 1)]
    peers += [sibling] + [at_y(step) for step in (-2, -1, 1, 2)]
    other = 2 * yhi + 1 - ylo
    peers += [device(x, y, (z + dz) % 8, c) for dz in range(1, 8)]
    peers += [device(x, other, (z + dz) % 8, c) for dz in range(1, 8)]
    barrier = pltpu.get_barrier_semaphore()
    for peer in peers:
        pl.semaphore_signal(barrier, inc=1, device_id=peer, device_id_type=MESH)
    pl.semaphore_wait(barrier, len(peers))

    def x_own(j):
        rows = pl.ds(pl.multiple_of((c * 4 + x) * 128, 128), 128)
        for m, ref in enumerate((gate_in, up_in)):
            def part(core):
                return ref.at[:, pl.ds(pl.multiple_of(core * HALF + j * 128, 128), 128)]
            dst = wbuf.at[j, rows, pl.ds(m * 128, 128)]
            for core in (0, 1):
                remote(part(core), dst, x_send.at[j], x_recv.at[j, 2 * c], device(right, y, z, core))
                remote(part(core), dst, x_send.at[j], x_recv.at[j, 2 - c], device(left, y, z, core))
            remote(part(1 - c), dst, x_send.at[j], x_recv.at[j, 2], sibling)
            pltpu.make_async_copy(part(c), dst, x_recv.at[j, 2]).start()

    def x_forward(j):
        wait(wbuf.at[j, pl.ds(0, 128)], x_recv.at[j, 0])
        rows = pl.ds(pl.multiple_of(left * 128, 128), 128)
        block = wbuf.at[j, rows]
        remote(block, block, f_send.at[j], x_recv.at[j, 2], device(right, y, z, c))
        wait(wbuf.at[j, pl.ds(0, 128)], x_recv.at[j, 1])
        rows = pl.ds(pl.multiple_of((4 + right) * 128, 128), 128)
        block = wbuf.at[j, rows]
        remote(block, block, f_send.at[j], x_recv.at[j, 2], device(left, y, z, c))

    def own(j, step):
        rows = pl.ds(pl.multiple_of(((y + 8 + step) % 8) * 64, 64), 64)
        return cbuf[j, rows, :]

    def multiply(j):
        wait(wbuf.at[j, pl.ds(0, 768)], x_recv.at[j, 2])
        cbuf[j] = jnp.dot(tok[...], wbuf[j], preferred_element_type=F32)
        first = own(j, 4).astype(BF16)
        s1[j, 0] = first[:, :128]
        s1[j, 1] = first[:, 128:]
        for way, step in ((0, 1), (1, -1)):
            remote(s1.at[j, way], r1.at[j, way], ch_send.at[j, way, 0], ch_recv.at[j, way, 0], at_y(step))

    def pass_on(j, k):
        for way, step in ((0, 1), (1, -1)):
            mine = own(j, step * (4 - k))
            if k == 1:
                wait(r1.at[j, way], ch_recv.at[j, way, 0])
                part = r1[j, way].astype(F32)
                if way == 0:
                    sb[j, way, 0, :, :128] = (mine[:, :128] + part).astype(BF16)
                    sb[j, way, 0, :, 128:] = mine[:, 128:].astype(BF16)
                else:
                    sb[j, way, 0, :, :128] = mine[:, :128].astype(BF16)
                    sb[j, way, 0, :, 128:] = (mine[:, 128:] + part).astype(BF16)
            else:
                wait(rb.at[j, way, k - 2], ch_recv.at[j, way, k - 1])
                sb[j, way, k - 1] = (mine + rb[j, way, k - 2].astype(F32)).astype(BF16)
            remote(
                sb.at[j, way, k - 1], rb.at[j, way, k - 1], ch_send.at[j, way, k], ch_recv.at[j, way, k], at_y(step)
            )

    def tile(j):
        return pl.ds(pl.multiple_of(c * HALF + j * 128, 128), 128)

    def piece(j, step):
        return hid.at[pl.ds(pl.multiple_of(((y + 8 + step) % 8) * 64, 64), 64), tile(j)]

    def finish(j):
        for way in (0, 1):
            wait(rb.at[j, way, 2], ch_recv.at[j, way, 3])
        total = own(j, 0) + rb[j, 0, 2].astype(F32) + rb[j, 1, 2].astype(F32)
        gate, up = total[:, :128], total[:, 128:]
        value = gate / (1.0 + jnp.exp(-gate)) * up
        hid[pl.ds(pl.multiple_of(y * 64, 64), 64), tile(j)] = value.astype(BF16)
        remote(piece(j, 0), piece(j, 0), h_send.at[j], h1.at[j, 0], at_y(2))
        remote(piece(j, 0), piece(j, 0), h_send.at[j], h1.at[j, 1], at_y(-2))

    def relay(j):
        wait(piece(j, 0), h1.at[j, 0])
        for step in (2, 1, -1):
            remote(piece(j, -2), piece(j, -2), h_send.at[j], h2.at[j], at_y(step))
        wait(piece(j, 0), h1.at[j, 1])
        for step in (1, -1):
            remote(piece(j, 2), piece(j, 2), h_send.at[j], h2.at[j], at_y(step))

    def share(j):
        wait(hid.at[pl.ds(0, 320), pl.ds(0, 128)], h2.at[j])
        block = hid.at[:, tile(j)]
        remote(block, block, hs_send.at[j], hs_recv.at[j], sibling)

    def down_rows(k, at):
        return pl.ds(pl.multiple_of(k * HALF + at * ROWS, 16), ROWS)

    def down_pair():
        for k in range(4):
            cols = pl.ds(k * 128, 128)
            dst = dbuf.at[down_rows(ylo, x), cols]
            theirs = down_in.at[:, pl.ds(pl.multiple_of((2 * k + 1 - ylo) * 128, 128), 128)]
            remote(theirs, dst, d_sem.at[0], d_sem.at[1], device(x, other, z, c))
            ours = down_in.at[:, pl.ds(pl.multiple_of((2 * k + ylo) * 128, 128), 128)]
            pltpu.make_async_copy(ours, dst, d_sem.at[1]).start()

    def down_own():
        wait(dbuf.at[pl.ds(0, 2 * ROWS)], d_sem.at[1])
        for k in (0, 1):
            block = dbuf.at[down_rows(k, x)]
            remote(block, block, d_sem.at[2], d_sem.at[3 if k == 0 else 5], device(right, y, z, c))
            remote(block, block, d_sem.at[2], d_sem.at[4 if k == 1 else 5], device(left, y, z, c))

    def down_forward():
        wait(dbuf.at[pl.ds(0, ROWS)], d_sem.at[3])
        block = dbuf.at[down_rows(0, left)]
        remote(block, block, d_sem.at[6], d_sem.at[5], device(right, y, z, c))
        wait(dbuf.at[pl.ds(0, ROWS)], d_sem.at[4])
        block = dbuf.at[down_rows(1, right)]
        remote(block, block, d_sem.at[6], d_sem.at[5], device(left, y, z, c))

    x_own(0)
    x_own(1)
    plane = 2 * yhi + z // 4
    tok_dst = tok.at[
        pl.ds(pl.multiple_of(ylo * 256, 256), 256), pl.ds(pl.multiple_of(c * 512 + (z % 4) * 128, 128), 128)
    ]
    for dz in (4, 3, 5, 2, 6, 1, 7):
        remote(tok_in, tok_dst, tok_sem.at[0], tok_sem.at[1], device(x, plane, (z + dz) % 8, c))

    @pl.when(plane == y)
    def _():
        pltpu.make_async_copy(tok_in, tok_dst, tok_sem.at[1]).start()

    @pl.when(plane != y)
    def _():
        remote(tok_in, tok_dst, tok_sem.at[2], tok_sem.at[1], device(x, plane, z, c))

    down_pair()
    x_forward(0)
    x_own(2)
    x_forward(1)
    x_own(3)
    half = tok.at[:, pl.ds(pl.multiple_of(c * 512, 512), 512)]
    wait(half, tok_sem.at[1])
    remote(half, half, tok_sem.at[3], tok_sem.at[4], sibling)
    wait(half, tok_sem.at[4])

    def tick(t, carry):
        def when(lo, hi, f, *args):
            @pl.when((t >= lo) & (t < hi))
            def _():
                f(*args)

        when(0, CHUNKS - 2, lambda: x_forward(t + 2))
        when(0, CHUNKS - 4, lambda: x_own(t + 4))
        when(CHUNKS - 4, CHUNKS - 3, down_own)
        when(0, CHUNKS, lambda: multiply(t))
        when(1, CHUNKS + 1, lambda: pass_on(t - 1, 2))
        when(2, CHUNKS + 2, lambda: finish(t - 2))
        when(3, CHUNKS + 3, lambda: relay(t - 3))
        when(4, CHUNKS + 4, lambda: share(t - 4))
        when(CHUNKS + 1, CHUNKS + 2, down_forward)
        when(0, CHUNKS, lambda: pass_on(t, 1))
        when(1, CHUNKS + 1, lambda: pass_on(t - 1, 3))
        return carry

    lax.fori_loop(0, CHUNKS + 2, tick, 0)
    relay(CHUNKS - 1)
    share(CHUNKS - 2)
    share(CHUNKS - 1)
    wait(dbuf.at[pl.ds(0, 4 * ROWS)], d_sem.at[5])

    def shared(j, carry):
        wait(hid.at[:, pl.ds(0, 128)], hs_recv.at[j])
        return carry

    lax.fori_loop(0, CHUNKS, shared, 0)

    for t in (0, 1):
        rows = pl.ds(t * 256, 256)
        for n in (0, 1):
            block = jnp.dot(hid[rows, :], dbuf[:, n * 256 : n * 256 + 256], preferred_element_type=F32)
            block = block.astype(BF16)
            for k in (2 * n, 2 * n + 1):
                osend[t, k] = block[:, (k - 2 * n) * 128 : (k - 2 * n) * 128 + 128]
                at = 2 * k + ylo
                here = jnp.logical_and(at == z, ylo == t)

                @pl.when(here)
                def _():
                    pltpu.make_async_copy(osend.at[t, k], orecv.at[z], o_sem.at[1]).start()

                @pl.when(jnp.logical_not(here))
                def _():
                    remote(osend.at[t, k], orecv.at[z], o_sem.at[0], o_sem.at[1], device(x, 2 * yhi + t, at, c))

    wait(orecv, o_sem.at[1])
    total = orecv[0].astype(F32)
    for k in range(1, 8):
        total = total + orecv[k].astype(F32)
    out_ref[...] = total.astype(BF16)

    wait(orecv.at[pl.ds(0, 7)], o_sem.at[0])

    @pl.when(ylo != z % 2)
    def _():
        wait(orecv.at[0], o_sem.at[0])

    wait(orecv.at[pl.ds(0, 7)], tok_sem.at[0])

    @pl.when(plane != y)
    def _():
        wait(orecv.at[0], tok_sem.at[2])

    wait(half, tok_sem.at[3])
    wait(dbuf.at[pl.ds(0, ROWS)], d_sem.at[0])
    wait(dbuf.at[pl.ds(0, 4 * ROWS)], d_sem.at[2])
    wait(dbuf.at[pl.ds(0, 2 * ROWS)], d_sem.at[6])

    def drain(j, carry):
        wait(wbuf.at[j, pl.ds(0, 640)], x_send.at[j])
        wait(wbuf.at[j, pl.ds(0, 256)], f_send.at[j])
        for way in (0, 1):
            wait(s1.at[j, way], ch_send.at[j, way, 0])
            for k in (1, 2, 3):
                wait(sb.at[j, way, k - 1], ch_send.at[j, way, k])
        wait(hid.at[pl.ds(0, 448), pl.ds(0, 128)], h_send.at[j])
        wait(hid.at[:, pl.ds(0, 128)], hs_send.at[j])
        return carry

    lax.fori_loop(0, CHUNKS, drain, 0)


def local(tokens, gate_weight, up_weight, down_weight):
    dma = pltpu.SemaphoreType.DMA
    J = CHUNKS
    return pl.pallas_call(
        kernel,
        out_shape=jax.ShapeDtypeStruct((256, 128), BF16),
        in_specs=[pl.BlockSpec(memory_space=pl.ANY)] * 4,
        out_specs=pl.BlockSpec(memory_space=pltpu.VMEM),
        scratch_shapes=[
            pltpu.VMEM((512, 1024), BF16),
            pltpu.VMEM((J, 1024, 256), BF16),
            pltpu.VMEM((J, 512, 256), F32),
            pltpu.VMEM((J, 2, 64, 128), BF16),
            pltpu.VMEM((J, 2, 64, 128), BF16),
            pltpu.VMEM((J, 2, 3, 64, 256), BF16),
            pltpu.VMEM((J, 2, 3, 64, 256), BF16),
            pltpu.VMEM((512, 2 * HALF), BF16),
            pltpu.VMEM((2 * HALF, 512), BF16),
            pltpu.VMEM((2, 4, 256, 128), BF16),
            pltpu.VMEM((8, 256, 128), BF16),
            dma((5,)),
            dma((J,)),
            dma((J, 3)),
            dma((J,)),
            dma((J, 2, 4)),
            dma((J, 2, 4)),
            dma((J,)),
            dma((J, 2)),
            dma((J,)),
            dma((J,)),
            dma((J,)),
            dma((7,)),
            dma((2,)),
        ],
        compiler_params=pltpu.CompilerParams(
            collective_id=0, has_side_effects=True, vmem_limit_bytes=48 << 20
        ),
        cost_estimate=pl.CostEstimate(flops=2 * 1409286144, bytes_accessed=4 << 20, transcendentals=114688),
    )(tokens, gate_weight, up_weight, down_weight)


def solution(mesh):
    in_specs = (
        P("gy", ("gz", "gx")),
        P(("gz", "gy"), "gx"),
        P(("gz", "gy"), "gx"),
        P(("gx", "gy"), "gz"),
    )
    out_specs = P("gy", ("gz", "gx"))
    return jax.shard_map(local, mesh=mesh, in_specs=in_specs, out_specs=out_specs, check_vma=False)
```

time: 324 us -> 117 us (0.36); the launches traced: 320 us -> 117 us
  waiting for transfers between devices: 245 us -> 0 us
  Pallas kernels: 0 us -> 112 us
  blocking collectives: 45.6 us -> 0 us
  between operations: 13.5 us -> 0.01 us
  matrix products: 12 us -> 0 us
    all_gather x3 -> x0, waiting for transfers between devices: 119 us -> none  [the longest x1 49.9 us: local(): lax.all_gather(up_weight, 'gy', axis=0, tiled=True)]
    pallas_call x0 -> x1, Pallas kernels: none -> 112 us  [local(): pl.pallas_call(kernel, out_shape=jax.ShapeDtypeStruct((256, 128), BF16),...]
    reduce_scatter x2 -> x0, waiting for transfers between devices: 87.7 us -> none  [the longest x1 47.3 us: local(): lax.psum_scatter(up_next, 'gz', scatter_dimension=0, tiled=True)]
    all_gather x2 -> x0, blocking collectives: 45.6 us -> none  [the longest x1 26.5 us: local(): token_block = lax.all_gather(tokens, 'gx', axis=1, tiled=True)]
    unnamed x7 -> x0, waiting for transfers between devices: 37.4 us -> none
    dot_general x3 -> x0, matrix products: 12 us -> none  [the longest x1 4.45 us: local(): jnp.dot(columns, lax.all_gather(gate_weight, 'gy', axis=0, tiled=True), p...]
  transfers between devices with their start and end apart: 6 -> 0, of which waited for: 6 -> 0; matrix products, arithmetic and copies ran while one was open for 3% -> 0% of each run, Pallas kernels for 0% -> 0%
where the time goes in v1:
time: 117 us
  Pallas kernels  112 us (96%)
  local copies, waits for them, and re-layouts  4.52 us (4%)
    pallas_call x1, Pallas kernels, local(): pl.pallas_call(kernel, out_shape=jax.ShapeDtypeStruct((256, 128), BF16),...  112 us
    unnamed x9, local copies, waits for them, and re-layouts  4.52 us

profile of v1, /device:TPU:1, one launch (start us, length us, event | category | flops | bytes accessed | tf_op | source)
XLA Modules:
  0.0 116.8 jit_solution(2273868622212823516)
XLA Ops:
  0.0 0.0 copy-start
  0.0 1.0 copy-done
  1.0 0.0 copy-start.1
  1.0 1.0 copy-done.1
  2.0 0.0 copy-start.2
  2.0 1.0 copy-done.2
  3.1 0.0 copy-start.3
  3.1 0.8 copy-done.3
  3.9 112.3 %shard_map.46 = bf16[256,128]{1,0:T(8,128)(2,1)S(1)} custom-call(bf16[256,128]{1,0:T(8,128)(2,1)S(1)} %copy-done.3, bf16[128,1792]{1,0:T(8,128)(2,1)S(1)} %copy-done, bf16[128,1792]{1,0:T(8,128)(2,1)S(1)} %copy-done.1, bf16[224,1024]{1,0:T(8,128)(2,1)S(1)} %copy-done.2), custom_call_target="tpu_custom_call" | custom-call | flops 2818572288 | bytes 4194304 | tf_op jit(solution)/shard_map/pallas_call | solution.py:283
  116.2 0.6 copy.6
Async XLA Ops:
  0.0 1.0 copy-start
  1.0 1.0 copy-start.1
  2.0 1.0 copy-start.2
  3.1 0.8 copy-start.3

commit v2 on v1

--- a/solution.py
+++ b/solution.py
@@ -11,6 +11,8 @@
 F32, BF16 = jnp.float32, jnp.bfloat16
 CHUNKS = 7
 HALF = 896
+GROUPS = 4
+LAG = 2
 ROWS = 224
 
 
@@ -32,7 +34,7 @@
 def kernel(
     tok_in, gate_in, up_in, down_in, out_ref,
     tok, wbuf, cbuf, s1, r1, sb, rb, hid, dbuf, osend, orecv,
-    tok_sem, x_send, x_recv, f_send, ch_send, ch_recv, h_send, h1, h2, hs_send, hs_recv, d_sem, o_sem,
+    tok_sem, t_recv, x_send, x_recv, f_send, ch_send, ch_recv, h_send, h1, h2, hs_send, hs_recv, d_sem, o_send, o_recv,
 ):
     z = lax.axis_index("gx")
     gy, gz = lax.axis_index("gy"), lax.axis_index("gz")
@@ -82,7 +84,7 @@
 
     def multiply(j):
         wait(wbuf.at[j, pl.ds(0, 768)], x_recv.at[j, 2])
-        cbuf[j] = jnp.dot(tok[...], wbuf[j], preferred_element_type=F32)
+        cbuf[j] = jnp.dot(tok[ylo], wbuf[j], preferred_element_type=F32)
         first = own(j, 4).astype(BF16)
         s1[j, 0] = first[:, :128]
         s1[j, 1] = first[:, 128:]
@@ -108,34 +110,38 @@
                 sb.at[j, way, k - 1], rb.at[j, way, k - 1], ch_send.at[j, way, k], ch_recv.at[j, way, k], at_y(step)
             )
 
-    def tile(j):
-        return pl.ds(pl.multiple_of(c * HALF + j * 128, 128), 128)
-
-    def piece(j, step):
-        return hid.at[pl.ds(pl.multiple_of(((y + 8 + step) % 8) * 64, 64), 64), tile(j)]
-
     def finish(j):
         for way in (0, 1):
             wait(rb.at[j, way, 2], ch_recv.at[j, way, 3])
         total = own(j, 0) + rb[j, 0, 2].astype(F32) + rb[j, 1, 2].astype(F32)
         gate, up = total[:, :128], total[:, 128:]
-        value = gate / (1.0 + jnp.exp(-gate)) * up
-        hid[pl.ds(pl.multiple_of(y * 64, 64), 64), tile(j)] = value.astype(BF16)
-        remote(piece(j, 0), piece(j, 0), h_send.at[j], h1.at[j, 0], at_y(2))
-        remote(piece(j, 0), piece(j, 0), h_send.at[j], h1.at[j, 1], at_y(-2))
-
-    def relay(j):
-        wait(piece(j, 0), h1.at[j, 0])
+        value = (gate / (1.0 + jnp.exp(-gate)) * up).astype(BF16)
+        for g in range(GROUPS):
+            hid[g, pl.ds(pl.multiple_of(y * 16, 16), 16), pl.ds(pl.multiple_of(c * HALF + j * 128, 128), 128)] = (
+                value[g * 16 : g * 16 + 16]
+            )
+
+    mine = pl.ds(pl.multiple_of(c * HALF, 128), HALF)
+
+    def piece(g, step):
+        return hid.at[g, pl.ds(pl.multiple_of(((y + 8 + step) % 8) * 16, 16), 16), mine]
+
+    def spread(g):
+        remote(piece(g, 0), piece(g, 0), h_send.at[g], h1.at[g, 0], at_y(2))
+        remote(piece(g, 0), piece(g, 0), h_send.at[g], h1.at[g, 1], at_y(-2))
+
+    def relay(g):
+        wait(piece(g, 0), h1.at[g, 0])
         for step in (2, 1, -1):
-            remote(piece(j, -2), piece(j, -2), h_send.at[j], h2.at[j], at_y(step))
-        wait(piece(j, 0), h1.at[j, 1])
+            remote(piece(g, -2), piece(g, -2), h_send.at[g], h2.at[g], at_y(step))
+        wait(piece(g, 0), h1.at[g, 1])
         for step in (1, -1):
-            remote(piece(j, 2), piece(j, 2), h_send.at[j], h2.at[j], at_y(step))
-
-    def share(j):
-        wait(hid.at[pl.ds(0, 320), pl.ds(0, 128)], h2.at[j])
-        block = hid.at[:, tile(j)]
-        remote(block, block, hs_send.at[j], hs_recv.at[j], sibling)
+            remote(piece(g, 2), piece(g, 2), h_send.at[g], h2.at[g], at_y(step))
+
+    def share(g):
+        wait(hid.at[0, pl.ds(0, 80), pl.ds(0, HALF)], h2.at[g])
+        block = hid.at[g, :, mine]
+        remote(block, block, hs_send.at[g], hs_recv.at[g], sibling)
 
     def down_rows(k, at):
         return pl.ds(pl.multiple_of(k * HALF + at * ROWS, 16), ROWS)
@@ -164,101 +170,148 @@
         block = dbuf.at[down_rows(1, right)]
         remote(block, block, d_sem.at[6], d_sem.at[5], device(left, y, z, c))
 
+    def tok_block(at):
+        at = (z + 8 + at) % 8
+        return tok.at[
+            at // 4,
+            pl.ds(pl.multiple_of(ylo * 256, 256), 256),
+            pl.ds(pl.multiple_of(c * 512 + (at % 4) * 128, 128), 128),
+        ]
+
+    def at_z(step):
+        return device(x, y, (z + 8 + step) % 8, c)
+
+    def cross(src, at):
+        @pl.when(((z + 8 + at) % 8) // 4 != ylo)
+        def _():
+            remote(src, tok_block(at), tok_sem.at[0], tok_sem.at[1], device(x, other, z, c))
+
+    def tok_first():
+        pltpu.make_async_copy(tok_in, tok_block(0), tok_sem.at[2]).start()
+        remote(tok_in, tok_block(0), tok_sem.at[3], t_recv.at[0], at_z(2))
+        remote(tok_in, tok_block(0), tok_sem.at[3], t_recv.at[1], at_z(-2))
+        cross(tok_in, 0)
+
+    def tok_relay():
+        wait(tok_block(0), t_recv.at[0])
+        for step, slot in ((-1, 2), (1, 3), (2, 4)):
+            remote(tok_block(-2), tok_block(-2), tok_sem.at[4], t_recv.at[slot], at_z(step))
+        cross(tok_block(-2), -2)
+        wait(tok_block(0), t_recv.at[1])
+        for step, slot in ((1, 5), (-1, 6)):
+            remote(tok_block(2), tok_block(2), tok_sem.at[4], t_recv.at[slot], at_z(step))
+        cross(tok_block(2), 2)
+
+    def tok_rows(plane):
+        return tok.at[
+            ylo, pl.ds(pl.multiple_of(plane * 256, 256), 256), pl.ds(pl.multiple_of(c * 512, 512), 512)
+        ]
+
+    def tok_mid():
+        for slot, at in ((2, -1), (5, 1), (3, -3), (6, 3), (4, -4)):
+            wait(tok_block(0), t_recv.at[slot])
+            cross(tok_block(at), at)
+        wait(tok_block(0), tok_sem.at[2])
+        remote(tok_rows(ylo), tok_rows(ylo), tok_sem.at[5], tok_sem.at[6], sibling)
+
+    def tok_last():
+        wait(tok_rows(0), tok_sem.at[1])
+        remote(tok_rows(1 - ylo), tok_rows(1 - ylo), tok_sem.at[5], tok_sem.at[6], sibling)
+        wait(tok.at[0, :, pl.ds(0, 512)], tok_sem.at[6])
+
+    tok_first()
     x_own(0)
     x_own(1)
-    plane = 2 * yhi + z // 4
-    tok_dst = tok.at[
-        pl.ds(pl.multiple_of(ylo * 256, 256), 256), pl.ds(pl.multiple_of(c * 512 + (z % 4) * 128, 128), 128)
-    ]
-    for dz in (4, 3, 5, 2, 6, 1, 7):
-        remote(tok_in, tok_dst, tok_sem.at[0], tok_sem.at[1], device(x, plane, (z + dz) % 8, c))
-
-    @pl.when(plane == y)
-    def _():
-        pltpu.make_async_copy(tok_in, tok_dst, tok_sem.at[1]).start()
-
-    @pl.when(plane != y)
-    def _():
-        remote(tok_in, tok_dst, tok_sem.at[2], tok_sem.at[1], device(x, plane, z, c))
-
     down_pair()
+    x_own(2)
+    x_own(3)
+    tok_relay()
+    x_own(4)
     x_forward(0)
-    x_own(2)
+    x_own(5)
+    tok_mid()
+    x_own(6)
     x_forward(1)
-    x_own(3)
-    half = tok.at[:, pl.ds(pl.multiple_of(c * 512, 512), 512)]
-    wait(half, tok_sem.at[1])
-    remote(half, half, tok_sem.at[3], tok_sem.at[4], sibling)
-    wait(half, tok_sem.at[4])
+    tok_last()
+    x_forward(2)
 
     def tick(t, carry):
-        def when(lo, hi, f, *args):
+        def when(lo, hi, f):
             @pl.when((t >= lo) & (t < hi))
             def _():
-                f(*args)
-
-        when(0, CHUNKS - 2, lambda: x_forward(t + 2))
-        when(0, CHUNKS - 4, lambda: x_own(t + 4))
-        when(CHUNKS - 4, CHUNKS - 3, down_own)
+                f()
+
+        when(0, CHUNKS - 3, lambda: x_forward(t + 3))
+        when(CHUNKS - 3, CHUNKS - 2, down_own)
+        when(13, 14, down_forward)
+        when(4 * LAG, CHUNKS + 4 * LAG, lambda: finish(t - 4 * LAG))
+        when(3 * LAG, CHUNKS + 3 * LAG, lambda: pass_on(t - 3 * LAG, 3))
+        when(2 * LAG, CHUNKS + 2 * LAG, lambda: pass_on(t - 2 * LAG, 2))
+        when(LAG, CHUNKS + LAG, lambda: pass_on(t - LAG, 1))
         when(0, CHUNKS, lambda: multiply(t))
-        when(1, CHUNKS + 1, lambda: pass_on(t - 1, 2))
-        when(2, CHUNKS + 2, lambda: finish(t - 2))
-        when(3, CHUNKS + 3, lambda: relay(t - 3))
-        when(4, CHUNKS + 4, lambda: share(t - 4))
-        when(CHUNKS + 1, CHUNKS + 2, down_forward)
-        when(0, CHUNKS, lambda: pass_on(t, 1))
-        when(1, CHUNKS + 1, lambda: pass_on(t - 1, 3))
         return carry
 
-    lax.fori_loop(0, CHUNKS + 2, tick, 0)
-    relay(CHUNKS - 1)
-    share(CHUNKS - 2)
-    share(CHUNKS - 1)
+    lax.fori_loop(0, CHUNKS + 4 * LAG, tick, 0)
+    for g in range(GROUPS):
+        spread(g)
     wait(dbuf.at[pl.ds(0, 4 * ROWS)], d_sem.at[5])
 
-    def shared(j, carry):
-        wait(hid.at[:, pl.ds(0, 128)], hs_recv.at[j])
+    def output(g):
+        wait(hid.at[0, :, pl.ds(0, HALF)], hs_recv.at[g])
+        for n in (0, 1):
+            block = jnp.dot(hid[g], dbuf[:, n * 256 : n * 256 + 256], preferred_element_type=F32)
+            osend[g, n] = block.astype(BF16)
+            for i in (0, 1):
+                for t in (0, 1):
+                    at = 2 * (2 * n + i) + ylo
+                    src = osend.at[g, n, pl.ds(t * 64, 64), pl.ds(i * 128, 128)]
+                    here = jnp.logical_and(at == z, ylo == t)
+
+                    @pl.when(here)
+                    def _():
+                        pltpu.make_async_copy(src, orecv.at[g, z], o_recv.at[g]).start()
+
+                    @pl.when(jnp.logical_not(here))
+                    def _():
+                        remote(src, orecv.at[g, z], o_send.at[g], o_recv.at[g], device(x, 2 * yhi + t, at, c))
+
+    def last(t, carry):
+        def when(lo, f):
+            @pl.when((t >= lo) & (t < lo + GROUPS))
+            def _():
+                f()
+
+        when(0, lambda: relay(t))
+        when(1, lambda: share(t - 1))
+        when(2, lambda: output(t - 2))
         return carry
 
-    lax.fori_loop(0, CHUNKS, shared, 0)
-
-    for t in (0, 1):
-        rows = pl.ds(t * 256, 256)
-        for n in (0, 1):
-            block = jnp.dot(hid[rows, :], dbuf[:, n * 256 : n * 256 + 256], preferred_element_type=F32)
-            block = block.astype(BF16)
-            for k in (2 * n, 2 * n + 1):
-                osend[t, k] = block[:, (k - 2 * n) * 128 : (k - 2 * n) * 128 + 128]
-                at = 2 * k + ylo
-                here = jnp.logical_and(at == z, ylo == t)
-
-                @pl.when(here)
-                def _():
-                    pltpu.make_async_copy(osend.at[t, k], orecv.at[z], o_sem.at[1]).start()
-
-                @pl.when(jnp.logical_not(here))
-                def _():
-                    remote(osend.at[t, k], orecv.at[z], o_sem.at[0], o_sem.at[1], device(x, 2 * yhi + t, at, c))
-
-    wait(orecv, o_sem.at[1])
-    total = orecv[0].astype(F32)
-    for k in range(1, 8):
-        total = total + orecv[k].astype(F32)
-    out_ref[...] = total.astype(BF16)
-
-    wait(orecv.at[pl.ds(0, 7)], o_sem.at[0])
-
-    @pl.when(ylo != z % 2)
-    def _():
-        wait(orecv.at[0], o_sem.at[0])
-
-    wait(orecv.at[pl.ds(0, 7)], tok_sem.at[0])
-
-    @pl.when(plane != y)
-    def _():
-        wait(orecv.at[0], tok_sem.at[2])
-
-    wait(half, tok_sem.at[3])
+    lax.fori_loop(0, GROUPS + 2, last, 0)
+    for g in range(GROUPS):
+        wait(orecv.at[g], o_recv.at[g])
+        total = orecv[g, 0].astype(F32)
+        for k in range(1, 8):
+            total = total + orecv[g, k].astype(F32)
+        total = total.astype(BF16)
+        for k in range(4):
+            out_ref[k * 64 + g * 16 : k * 64 + g * 16 + 16, :] = total[k * 16 : k * 16 + 16]
+
+    def left_late(g, carry):
+        wait(orecv.at[0, pl.ds(0, 7)], o_send.at[g])
+
+        @pl.when(ylo != z % 2)
+        def _():
+            wait(orecv.at[0, 0], o_send.at[g])
+
+        wait(hid.at[0, pl.ds(0, 112), pl.ds(0, HALF)], h_send.at[g])
+        wait(hid.at[0, :, pl.ds(0, HALF)], hs_send.at[g])
+        return carry
+
+    lax.fori_loop(0, GROUPS, left_late, 0)
+    wait(tok.at[0, :, pl.ds(0, 256)], tok_sem.at[0])
+    wait(tok.at[0, pl.ds(0, 256), pl.ds(0, 256)], tok_sem.at[3])
+    wait(tok.at[0, pl.ds(0, 256), pl.ds(0, 640)], tok_sem.at[4])
+    wait(tok.at[0, :, pl.ds(0, 512)], tok_sem.at[5])
     wait(dbuf.at[pl.ds(0, ROWS)], d_sem.at[0])
     wait(dbuf.at[pl.ds(0, 4 * ROWS)], d_sem.at[2])
     wait(dbuf.at[pl.ds(0, 2 * ROWS)], d_sem.at[6])
@@ -270,8 +323,6 @@
             wait(s1.at[j, way], ch_send.at[j, way, 0])
             for k in (1, 2, 3):
                 wait(sb.at[j, way, k - 1], ch_send.at[j, way, k])
-        wait(hid.at[pl.ds(0, 448), pl.ds(0, 128)], h_send.at[j])
-        wait(hid.at[:, pl.ds(0, 128)], hs_send.at[j])
         return carry
 
     lax.fori_loop(0, CHUNKS, drain, 0)
@@ -286,33 +337,35 @@
         in_specs=[pl.BlockSpec(memory_space=pl.ANY)] * 4,
         out_specs=pl.BlockSpec(memory_space=pltpu.VMEM),
         scratch_shapes=[
-            pltpu.VMEM((512, 1024), BF16),
+            pltpu.VMEM((2, 512, 1024), BF16),
             pltpu.VMEM((J, 1024, 256), BF16),
             pltpu.VMEM((J, 512, 256), F32),
             pltpu.VMEM((J, 2, 64, 128), BF16),
             pltpu.VMEM((J, 2, 64, 128), BF16),
             pltpu.VMEM((J, 2, 3, 64, 256), BF16),
             pltpu.VMEM((J, 2, 3, 64, 256), BF16),
-            pltpu.VMEM((512, 2 * HALF), BF16),
+            pltpu.VMEM((GROUPS, 128, 2 * HALF), BF16),
             pltpu.VMEM((2 * HALF, 512), BF16),
-            pltpu.VMEM((2, 4, 256, 128), BF16),
-            pltpu.VMEM((8, 256, 128), BF16),
-            dma((5,)),
+            pltpu.VMEM((GROUPS, 2, 128, 256), BF16),
+            pltpu.VMEM((GROUPS, 8, 64, 128), BF16),
+            dma((7,)),
+            dma((7,)),
             dma((J,)),
             dma((J, 3)),
             dma((J,)),
             dma((J, 2, 4)),
             dma((J, 2, 4)),
-            dma((J,)),
-            dma((J, 2)),
-            dma((J,)),
-            dma((J,)),
-            dma((J,)),
+            dma((GROUPS,)),
+            dma((GROUPS, 2)),
+            dma((GROUPS,)),
+            dma((GROUPS,)),
+            dma((GROUPS,)),
             dma((7,)),
-            dma((2,)),
+            dma((GROUPS,)),
+            dma((GROUPS,)),
         ],
         compiler_params=pltpu.CompilerParams(
-            collective_id=0, has_side_effects=True, vmem_limit_bytes=48 << 20
+            collective_id=0, has_side_effects=True, vmem_limit_bytes=62 << 20
         ),
         cost_estimate=pl.CostEstimate(flops=2 * 1409286144, bytes_accessed=4 << 20, transcendentals=114688),
     )(tokens, gate_weight, up_weight, down_weight)

time: 117 us -> 95.5 us (0.82)
  Pallas kernels: 112 us -> 93.9 us
  local copies, waits for them, and re-layouts: 4.52 us -> 1.47 us
    pallas_call x1, Pallas kernels: 112 us -> 93.9 us  [local(): pl.pallas_call(kernel, out_shape=jax.ShapeDtypeStruct((256, 128), BF16),...]
    unnamed x9 -> x1, local copies, waits for them, and re-layouts: 4.52 us -> 1.47 us
where the time goes in v2:
time: 95.5 us; the launch traced here: 95.4 us
  Pallas kernels  93.9 us (98%)
  local copies, waits for them, and re-layouts  1.47 us (2%)
    pallas_call x1, Pallas kernels, local(): pl.pallas_call(kernel, out_shape=jax.ShapeDtypeStruct((256, 128), BF16),...  93.9 us

profile of v2, /device:TPU:1, one launch (start us, length us, event | category | flops | bytes accessed | tf_op | source)
XLA Modules:
  0.0 95.4 jit_solution(1403123615465476748)
XLA Ops:
  0.0 93.9 %shard_map.46 = bf16[256,128]{1,0:T(8,128)(2,1)} custom-call(bf16[256,128]{1,0:T(8,128)(2,1)} %tok_in.1, bf16[128,1792]{1,0:T(8,128)(2,1)} %gate_in.1, bf16[128,1792]{1,0:T(8,128)(2,1)} %up_in.1, bf16[224,1024]{1,0:T(8,128)(2,1)} %down_in.1), custom_call_target="tpu_custom_call" | custom-call | flops 2818572288 | bytes 4194304 | tf_op jit(solution)/shard_map/pallas_call | solution.py:334
  93.9 1.5 %copy.6 = bf16[256,128]{1,0:T(8,128)(2,1)} copy(bf16[256,128]{1,0:T(8,128)(2,1)} %shard_map.46) | data formatting | bytes 131072

commit v3 on v2

--- a/solution.py
+++ b/solution.py
@@ -12,7 +12,7 @@
 CHUNKS = 7
 HALF = 896
 GROUPS = 4
-LAG = 2
+LAG = 3
 ROWS = 224
 
 
@@ -131,12 +131,13 @@
         remote(piece(g, 0), piece(g, 0), h_send.at[g], h1.at[g, 1], at_y(-2))
 
     def relay(g):
-        wait(piece(g, 0), h1.at[g, 0])
-        for step in (2, 1, -1):
-            remote(piece(g, -2), piece(g, -2), h_send.at[g], h2.at[g], at_y(step))
-        wait(piece(g, 0), h1.at[g, 1])
-        for step in (1, -1):
-            remote(piece(g, 2), piece(g, 2), h_send.at[g], h2.at[g], at_y(step))
+        far = 2 - 4 * c
+        for way in (0, 1):
+            wait(piece(g, 0), h1.at[g, way])
+        remote(piece(g, -far), piece(g, -far), h_send.at[g], h2.at[g], at_y(far))
+        for block in (-2, 2):
+            for step in (1, -1):
+                remote(piece(g, block), piece(g, block), h_send.at[g], h2.at[g], at_y(step))
 
     def share(g):
         wait(hid.at[0, pl.ds(0, 80), pl.ds(0, HALF)], h2.at[g])
@@ -193,13 +194,13 @@
         cross(tok_in, 0)
 
     def tok_relay():
-        wait(tok_block(0), t_recv.at[0])
-        for step, slot in ((-1, 2), (1, 3), (2, 4)):
-            remote(tok_block(-2), tok_block(-2), tok_sem.at[4], t_recv.at[slot], at_z(step))
+        far = 2 - 4 * c
+        for way in (0, 1):
+            wait(tok_block(0), t_recv.at[way])
+        remote(tok_block(-far), tok_block(-far), tok_sem.at[4], t_recv.at[4], at_z(far))
+        for block, step, slot in ((-2, -1, 2), (2, 1, 5), (-2, 1, 3), (2, -1, 6)):
+            remote(tok_block(block), tok_block(block), tok_sem.at[4], t_recv.at[slot], at_z(step))
         cross(tok_block(-2), -2)
-        wait(tok_block(0), t_recv.at[1])
-        for step, slot in ((1, 5), (-1, 6)):
-            remote(tok_block(2), tok_block(2), tok_sem.at[4], t_recv.at[slot], at_z(step))
         cross(tok_block(2), 2)
 
     def tok_rows(plane):
@@ -225,14 +226,14 @@
     down_pair()
     x_own(2)
     x_own(3)
+    x_own(4)
     tok_relay()
-    x_own(4)
+    x_own(5)
+    x_own(6)
+    tok_mid()
     x_forward(0)
-    x_own(5)
-    tok_mid()
-    x_own(6)
+    tok_last()
     x_forward(1)
-    tok_last()
     x_forward(2)
 
     def tick(t, carry):
@@ -241,9 +242,9 @@
             def _():
                 f()
 
-        when(0, CHUNKS - 3, lambda: x_forward(t + 3))
+        when(0, 4, lambda: x_forward(t + 3))
         when(CHUNKS - 3, CHUNKS - 2, down_own)
-        when(13, 14, down_forward)
+        when(17, 18, down_forward)
         when(4 * LAG, CHUNKS + 4 * LAG, lambda: finish(t - 4 * LAG))
         when(3 * LAG, CHUNKS + 3 * LAG, lambda: pass_on(t - 3 * LAG, 3))
         when(2 * LAG, CHUNKS + 2 * LAG, lambda: pass_on(t - 2 * LAG, 2))

time: 95.5 us -> 94.7 us (level)
  no operation moved by 1% of the time
where the time goes in v3:
time: 94.7 us; the launch traced here: 94.6 us
  Pallas kernels  93.1 us (98%)
  local copies, waits for them, and re-layouts  1.47 us (2%)
    pallas_call x1, Pallas kernels, local(): pl.pallas_call(kernel, out_shape=jax.ShapeDtypeStruct((256, 128), BF16),...  93.1 us

profile of v3, /device:TPU:1, one launch (start us, length us, event | category | flops | bytes accessed | tf_op | source)
XLA Modules:
  0.0 94.6 jit_solution(3473552596670744566)
XLA Ops:
  0.0 93.1 %shard_map.46 = bf16[256,128]{1,0:T(8,128)(2,1)} custom-call(bf16[256,128]{1,0:T(8,128)(2,1)} %tok_in.1, bf16[128,1792]{1,0:T(8,128)(2,1)} %gate_in.1, bf16[128,1792]{1,0:T(8,128)(2,1)} %up_in.1, bf16[224,1024]{1,0:T(8,128)(2,1)} %down_in.1), custom_call_target="tpu_custom_call" | custom-call | flops 2818572288 | bytes 4194304 | tf_op jit(solution)/shard_map/pallas_call | solution.py:335
  93.1 1.5 %copy.6 = bf16[256,128]{1,0:T(8,128)(2,1)} copy(bf16[256,128]{1,0:T(8,128)(2,1)} %shard_map.46) | data formatting | bytes 131072
